TPU v7x, 256 devices: a whole 4x4x8 slice. The times are simulated.
256 devices in a mesh: gx: 8 (over x, core), gy: 32 (over z, y).
Axes of the slice: x: 4, y: 4, z: 8, core: 2. Of those that a mesh axis runs over, the one named last changes fastest.
Arguments:
- source: float32 [128, 512, 256], P('gx', 'gy'), may hold values from -8 to 8
- conductivity: float32 [128, 512, 256], P('gx', 'gy'), may hold values from 1 to 10
- guess: float32 [128, 512, 256], P('gx', 'gy'), may hold values from -6 to 6
Outputs:
- updated: float32 [128, 512, 256], P('gx', 'gy')
All inputs are finite; a program needn't handle non-finite values.
Results may differ from a plain program's by a relative error of at most 0.0003.
Values sent between devices are 32-bit elements; how exact they have to be, the bound alone decides.
A program may use at most 128 MiB of HBM per device.

v0:
```python
import jax
import jax.numpy as jnp
from jax import lax
from jax.experimental import pallas as pl
from jax.experimental.pallas import tpu as pltpu
from jax.sharding import PartitionSpec as P

MESH = pl.DeviceIdType.MESH
F32, BF16 = jnp.float32, jnp.bfloat16
OMEGA = 0.8
GX, GY, NYC, NZC = 8, 32, 4, 8
EIGHT = [(0, 1), (0, -1), (1, 1), (1, -1), (-1, 1), (-1, -1), (1, 0), (-1, 0)]


def harmonic(a, b):
    return 2.0 * a * b / (a + b)


def mm(a, m):
    hi = a.astype(BF16)
    lo = (a - hi.astype(F32)).astype(BF16)
    return jnp.dot(hi, m, preferred_element_type=F32) + jnp.dot(lo, m, preferred_element_type=F32)


def zp(s):
    if len(s) == 1:
        return (pltpu.roll(s[0], 127, 1),)
    last = lax.broadcasted_iota(jnp.int32, s[0].shape, 1) == 127
    a, b = pltpu.roll(s[0], 127, 1), pltpu.roll(s[1], 127, 1)
    return (jnp.where(last, b, a), jnp.where(last, a, b))


def zm(s):
    if len(s) == 1:
        return (pltpu.roll(s[0], 1, 1),)
    first = lax.broadcasted_iota(jnp.int32, s[0].shape, 1) == 0
    a, b = pltpu.roll(s[0], 1, 1), pltpu.roll(s[1], 1, 1)
    return (jnp.where(first, b, a), jnp.where(first, a, b))


def yp(s):
    return tuple(pltpu.roll(a, a.shape[0] - 1, 0) for a in s)


def ym(s):
    return tuple(pltpu.roll(a, 1, 0) for a in s)


def each(f, *slabs):
    return tuple(f(*a) for a in zip(*slabs))


def get(ref, x):
    if len(ref.shape) == 4:
        return (ref[x, 0], ref[x, 1])
    return (ref[x],)


def put(ref, x, s):
    if len(ref.shape) == 4:
        ref[x, 0] = s[0]
        ref[x, 1] = s[1]
    else:
        ref[x] = s[0]


def add(a, b):
    return each(lambda p, q: p + q, a, b)


def sub(a, b):
    return each(lambda p, q: p - q, a, b)


def mul(a, b):
    return each(lambda p, q: p * q, a, b)


def coefficients(c_ref, cx_ref, cy_ref, cz_ref, w_ref, slabs, unroll):
    c = get(c_ref, 0)
    n = get(c_ref, 1)
    first = each(harmonic, c, n)
    put(cx_ref, 0, first)

    def body(x, carry):
        c, before = carry
        n = get(c_ref, x + 1)
        ex = each(harmonic, c, n)
        ey = each(harmonic, c, yp(c))
        ez = each(harmonic, c, zp(c))
        d = add(add(add(ex, before), add(ey, ym(ey))), add(ez, zm(ez)))
        put(cx_ref, x, ex)
        put(cy_ref, x, ey)
        put(cz_ref, x, ez)
        put(w_ref, x, each(lambda p: OMEGA / p, d))
        return n, ex

    lax.fori_loop(1, slabs - 1, body, (n, first), unroll=unroll)


def flux_loop(v_ref, b_ref, cx_ref, cy_ref, cz_ref, lo, hi, emit, unroll):
    v = get(v_ref, lo)
    before = mul(get(cx_ref, lo - 1), sub(v, get(v_ref, lo - 1)))

    def body(x, carry):
        v, before = carry
        n = get(v_ref, x + 1)
        tx = mul(get(cx_ref, x), sub(n, v))
        ty = mul(get(cy_ref, x), sub(yp(v), v))
        tz = mul(get(cz_ref, x), sub(zp(v), v))
        r = add(add(sub(tx, before), sub(ty, ym(ty))), sub(tz, zm(tz)))
        emit(x, v, add(get(b_ref, x), r))
        return n, tx

    lax.fori_loop(lo, hi, body, (v, before), unroll=unroll)


def sweep(v_ref, to_ref, b_ref, cx_ref, cy_ref, cz_ref, w_ref, lo, hi, unroll):
    def emit(x, v, r):
        put(to_ref, x, add(v, mul(get(w_ref, x), r)))

    flux_loop(v_ref, b_ref, cx_ref, cy_ref, cz_ref, lo, hi, emit, unroll)


def lane(shape):
    return lax.broadcasted_iota(jnp.int32, shape, len(shape) - 1)


def three_zp(v):
    return jnp.where(lane(v.shape) % 32 == 31, pltpu.roll(v, 31, 2), pltpu.roll(v, 127, 2))


def three_zm(v):
    return jnp.where(lane(v.shape) % 32 == 0, pltpu.roll(v, 97, 2), pltpu.roll(v, 1, 2))


def three_xp(v):
    r = pltpu.roll(v, 64, 2)
    return jnp.where(lane(v.shape) < 64, r, pltpu.roll(r, GX - 1, 1))


def three_xm(v):
    r = pltpu.roll(v, 64, 2)
    return jnp.where(lane(v.shape) < 64, pltpu.roll(r, 1, 1), r)


def three_y(v):
    up, down = pltpu.roll(v, 96, 2), pltpu.roll(v, 32, 2)
    first = lane(v[1:-1].shape) % 64 < 32
    return (jnp.where(first, up[1:-1], down[2:]), jnp.where(first, up[:-2], down[1:-1]))


def four_zp(v):
    return pltpu.roll(v, 126, 2)


def four_zm(v):
    return pltpu.roll(v, 2, 2)


def four_xp(v):
    return pltpu.roll(v, GX - 1, 1)


def four_xm(v):
    return pltpu.roll(v, 1, 1)


def four_y(v):
    return v[2:], v[:-2]


THREE = (three_xp, three_xm, three_y, three_zp, three_zm)
FOUR = (four_xp, four_xm, four_y, four_zp, four_zm)
CH = 4


def wrap_rows(ref):
    ref[0] = ref[GY]
    ref[GY + 1] = ref[1]


def whole_coefficients(level, c_ref, k_ref):
    xp, xm, y, zplus, zminus = level

    def body(i, carry):
        g = i * CH
        ext = c_ref[pl.ds(g, CH + 2)]
        c = ext[1:-1]
        up, down = y(ext)
        ex = harmonic(c, xp(c))
        ez = harmonic(c, zplus(c))
        ey, wy = harmonic(c, up), harmonic(down, c)
        wx, wz = xm(ex), zminus(ez)
        d = (ex + wx) + (ey + wy) + (ez + wz)
        for j, value in enumerate((ex, wx, ey, wy, ez, wz, d, OMEGA / d)):
            k_ref[j, pl.ds(g, CH)] = value
        return carry

    lax.fori_loop(0, GY // CH, body, 0, unroll=True)


def whole_sum(level, v_ref, k_ref, emit):
    xp, xm, y, zplus, zminus = level

    def body(i, carry):
        g = i * CH
        ext = v_ref[pl.ds(g, CH + 2)]
        v = ext[1:-1]
        up, down = y(ext)
        k = [k_ref[j, pl.ds(g, CH)] for j in range(6)]
        s = (k[0] * xp(v) + k[1] * xm(v)) + (k[2] * up + k[3] * down)
        emit(g, v, s + (k[4] * zplus(v) + k[5] * zminus(v)))
        return carry

    lax.fori_loop(0, GY // CH, body, 0, unroll=True)


def whole_sweep(level, v_ref, to_ref, b_ref, k_ref):
    def emit(g, v, s):
        to_ref[pl.ds(g + 1, CH)] = (1.0 - OMEGA) * v + k_ref[7, pl.ds(g, CH)] * (b_ref[pl.ds(g + 1, CH)] + s)

    whole_sum(level, v_ref, k_ref, emit)
    wrap_rows(to_ref)


def coarsen_lanes(v):
    s = v + pltpu.roll(v, 64, 2)
    s = s + pltpu.roll(s, 32, 2)
    return s + jnp.where(lane(v.shape) % 2 == 0, pltpu.roll(s, 127, 2), pltpu.roll(s, 1, 2))


def kernel(
    src_ref, cond_ref, guess_ref, out_ref,
    V0, B0, C0, CX0, CY0, CZ0, W0, VA0, VB0, VH, TR, PE0, TP0,
    C1, CX1, CY1, CZ1, W1, B1, VA1, VB1, R1, TP1,
    C2, CX2, CY2, CZ2, W2, B2, VA2, VB2, R2, B2H, V2H,
    C3, B3, V3A, V3B, K3, C4, B4, V4A, V4B, K4,
    MR, M3, MP1, MP2, MP3,
    lsem, e0s, e0r, c1s, c1r, b1s, b1r, h0s, h0r, h2s, h2r, cas, car, cbs, cbr, bas, bar, bbs, bbr,
):
    gx, gy = lax.axis_index("gx"), lax.axis_index("gy")
    yc, zc = lax.rem(gy, NYC), lax.div(gy, NYC)

    def beside(dx, dy):
        return (lax.rem(gx + dx + GX, GX), lax.rem(gy + dy + GY, GY))

    def in_plane(k):
        return (lax.rem(gx + lax.div(k, NYC), GX), zc * NYC + lax.rem(yc + lax.rem(k, NYC), NYC))

    def along_z(k):
        return (gx, lax.rem(zc + k, NZC) * NYC + yc)

    def remote(src, dst, send, recv, device):
        return pltpu.make_async_remote_copy(
            src_ref=src, dst_ref=dst, send_sem=send, recv_sem=recv, device_id=device, device_id_type=MESH
        )

    loads = []
    for i, (ref, to) in enumerate(((cond_ref, C0), (guess_ref, V0), (src_ref, B0))):
        for h in range(2):
            loads.append(
                pltpu.make_async_copy(
                    ref.at[:, :, pl.ds(128 * h, 128)],
                    to.at[pl.ds(3, 16), h, pl.ds(4, 16), :],
                    lsem.at[2 * i + h],
                )
            )
    for copy in loads:
        copy.start()

    barrier = pltpu.get_barrier_semaphore()
    for dx, dy in EIGHT:
        pl.semaphore_signal(barrier, inc=1, device_id=beside(dx, dy), device_id_type=MESH)

    def greet_plane(k, carry):
        pl.semaphore_signal(barrier, inc=1, device_id=in_plane(k), device_id_type=MESH)
        return carry

    def greet_z(k, carry):
        pl.semaphore_signal(barrier, inc=1, device_id=along_z(k), device_id_type=MESH)
        return carry

    lax.fori_loop(1, GX * NYC, greet_plane, 0)
    lax.fori_loop(1, NZC, greet_z, 0)

    def matrix(rows, columns, rule):
        r = lax.broadcasted_iota(jnp.int32, (rows, columns), 0)
        c = lax.broadcasted_iota(jnp.int32, (rows, columns), 1)
        return jnp.where(rule(r, c), 1.0, 0.0).astype(BF16)

    MR[0:256] = matrix(256, 128, lambda r, c: r // 2 == c)
    MR[256:384] = matrix(128, 128, lambda r, c: r // 2 == c % 64)
    M3[...] = matrix(128, 128, lambda r, c: (r < 64) & (r // 2 == c % 32))
    MP1[...] = matrix(128, 256, lambda r, c: r == c // 2)
    MP2[...] = matrix(128, 128, lambda r, c: r == c // 2)
    MP3[...] = matrix(128, 512, lambda r, c: (r // 32 == c // 128) & (r % 32 == (c % 64) // 2))

    for copy in loads:
        copy.wait()
    pl.semaphore_wait(barrier, len(EIGHT) + GX * NYC - 1 + NZC - 1)

    def edge(base, extent, step, width):
        if step == 0:
            return base, base, extent
        if step == 1:
            return base + extent - width, base - width, width
        return base, base + extent, width

    def block_copy(ref, base, extent, step, width, send, recv):
        sx, tx, nx = edge(base[0], extent, step[0], width)
        sy, ty, ny = edge(base[1], extent, step[1], width)
        if len(ref.shape) == 4:
            src, dst = ref.at[pl.ds(sx, nx), :, pl.ds(sy, ny), :], ref.at[pl.ds(tx, nx), :, pl.ds(ty, ny), :]
        else:
            src, dst = ref.at[pl.ds(sx, nx), pl.ds(sy, ny), :], ref.at[pl.ds(tx, nx), pl.ds(ty, ny), :]
        return remote(src, dst, send, recv, beside(*step))

    def exchange(ref, base, extent, width, send, recv):
        return [block_copy(ref, base, extent, o, width, send.at[i], recv.at[i]) for i, o in enumerate(EIGHT)]

    e0c = exchange(C0, (3, 4), 16, 3, e0s.at[0], e0r.at[0])
    e0v = exchange(V0, (3, 4), 16, 3, e0s.at[1], e0r.at[1])
    e0b = exchange(B0, (3, 4), 16, 2, e0s.at[2], e0r.at[2])
    for copies in (e0c, e0v, e0b):
        for copy in copies:
            copy.start()

    def restrict_zero(ref, scale):
        pairs = [
            jnp.concatenate([ref[3 + 2 * k, h, 4:20] + ref[4 + 2 * k, h, 4:20] for h in range(2)], axis=1)
            for k in range(8)
        ]
        TR[0:8, 0:16] = mm(jnp.concatenate(pairs, axis=0), MR[0:256]).reshape(8, 16, 128)
        return (TR[0:8, pl.ds(0, 8, stride=2), :] + TR[0:8, pl.ds(1, 8, stride=2), :]) * scale

    def restrict_one(ref, x0, count, y0, rows, scale):
        pairs = [ref[x0 + 2 * k, y0 : y0 + rows] + ref[x0 + 1 + 2 * k, y0 : y0 + rows] for k in range(count)]
        TR[0:count, 0:rows] = mm(jnp.concatenate(pairs, axis=0), MR[256:384]).reshape(count, rows, 128)
        half = rows // 2
        return (TR[0:count, pl.ds(0, half, stride=2), :] + TR[0:count, pl.ds(1, half, stride=2), :]) * scale

    def restrict_two(ref, scale):
        pairs = jnp.concatenate([ref[4] + ref[5], ref[6] + ref[7]], axis=0)
        s = mm(pairs, M3[...]) * scale
        group = lax.broadcasted_iota(jnp.int32, (1, 128), 1) // 32
        row = jnp.zeros((1, 128), F32)
        for g in range(4):
            at = 16 * (g // 2) + 4 + 2 * (g % 2)
            row = jnp.where(group == g, s[at : at + 1] + s[at + 1 : at + 2], row)
        return row

    def plane_copy(ref, k, send, recv):
        part = ref.at[gy + 1, pl.ds(gx, 1), :]
        return remote(part, part, send.at[k], recv.at[k], in_plane(k))

    def z_copy(ref, k, send, recv):
        part = ref.at[pl.ds(zc * NYC + 1, NYC)]
        return remote(part, part, send.at[k], recv.at[k], along_z(k))

    def start_plane(ref, send, recv):
        def go(k, carry):
            plane_copy(ref, k, send, recv).start()
            return carry

        lax.fori_loop(1, GX * NYC, go, 0)

    def landed_plane(ref, send, recv):
        def go(k, carry):
            plane_copy(ref, k, send, recv).wait_recv()
            return carry

        lax.fori_loop(1, GX * NYC, go, 0)

    def start_z(ref, send, recv):
        for k in range(1, NZC):
            z_copy(ref, k, send, recv).start()

    def landed_z(ref, send, recv):
        for k in range(1, NZC):
            z_copy(ref, k, send, recv).wait_recv()

    def sent(ref, plane_send, plane_recv, z_send, z_recv):
        def go(k, carry):
            plane_copy(ref, k, plane_send, plane_recv).wait_send()
            return carry

        lax.fori_loop(1, GX * NYC, go, 0)
        for k in range(1, NZC):
            z_copy(ref, k, z_send, z_recv).wait_send()

    C1[8:16, 8:16] = restrict_zero(C0, 0.125 * 0.25)
    c1 = exchange(C1, (8, 8), 8, 8, c1s, c1r)
    for copy in c1:
        copy.start()
    C2[4:8, 4:8] = restrict_one(C1, 8, 4, 8, 8, 0.125 * 0.25)
    C3[gy + 1, pl.ds(gx, 1), :] = restrict_two(C2, 0.125 * 0.25)
    start_plane(C3, cas, car)

    for copy in e0c:
        copy.wait_recv()
    coefficients(C0, CX0, CY0, CZ0, W0, 22, 2)
    for copy in e0v + e0b:
        copy.wait_recv()
    zero = (B0, CX0, CY0, CZ0)
    sweep(V0, VA0, *zero, W0, 1, 21, 2)
    sweep(VA0, VB0, *zero, W0, 2, 20, 2)
    flux_loop(VB0, *zero, 3, 19, lambda x, v, r: put(VA0, x, r), 2)
    B1[8:16, 8:16] = restrict_zero(VA0, 0.125)
    b1 = exchange(B1, (8, 8), 8, 8, b1s, b1r)
    for copy in b1:
        copy.start()

    h0 = [
        remote(VB0.at[pl.ds(sx, nx), :, pl.ds(sy, ny), :], VH.at[pl.ds(tx, nx), :, pl.ds(ty, ny), :],
               h0s.at[i], h0r.at[i], beside(*o))
        for i, (o, (sx, tx, nx), (sy, ty, ny)) in enumerate((
            ((0, 1), (3, 3, 16), (18, 2, 1)),
            ((0, -1), (3, 3, 16), (5, 21, 1)),
            ((1, 0), (17, 1, 1), (4, 4, 16)),
            ((-1, 0), (4, 20, 1), (4, 4, 16)),
        ))
    ]
    for copy in h0:
        copy.start()

    landed_plane(C3, cas, car)
    start_z(C3, cbs, cbr)

    for copy in c1:
        copy.wait_recv()
    coefficients(C1, CX1, CY1, CZ1, W1, 24, 2)
    for k in range(3):
        C2[4 * k : 4 * k + 4, 0:12] = restrict_one(C1, 8 * k, 4, 0, 24, 0.125 * 0.25)
    coefficients(C2, CX2, CY2, CZ2, W2, 12, True)

    for copy in b1:
        copy.wait_recv()

    def from_zero(to_ref, b_ref, w_ref, lo, hi):
        to_ref[lo:hi] = w_ref[lo:hi] * b_ref[lo:hi]

    one = (B1, CX1, CY1, CZ1)
    from_zero(VA1, B1, W1, 2, 22)
    sweep(VA1, VB1, *one, W1, 3, 21, 2)
    flux_loop(VB1, *one, 4, 20, lambda x, v, r: put(R1, x, r), 2)
    B2[2:10, 0:12] = restrict_one(R1, 4, 8, 0, 24, 0.125)

    two = (B2, CX2, CY2, CZ2)
    from_zero(VA2, B2, W2, 2, 10)
    sweep(VA2, VB2, *two, W2, 3, 9, True)
    flux_loop(VB2, *two, 4, 8, lambda x, v, r: put(R2, x, r), True)
    B3[gy + 1, pl.ds(gx, 1), :] = restrict_two(R2, 0.125)
    start_plane(B3, bas, bar)
    B2H[4:8, 4:8] = B2[4:8, 4:8]
    V2H[4:8, 4:8] = VB2[4:8, 4:8]
    h2 = exchange(B2H, (4, 4), 4, 4, h2s.at[0], h2r.at[0]) + exchange(V2H, (4, 4), 4, 4, h2s.at[1], h2r.at[1])
    for copy in h2:
        copy.start()

    landed_z(C3, cbs, cbr)
    wrap_rows(C3)
    whole_coefficients(THREE, C3, K3)
    C4[1 : GY + 1] = coarsen_lanes(C3[1 : GY + 1]) * (0.125 * 0.25)
    wrap_rows(C4)
    whole_coefficients(FOUR, C4, K4)

    landed_plane(B3, bas, bar)
    start_z(B3, bbs, bbr)
    landed_z(B3, bbs, bbr)

    V3A[1 : GY + 1] = K3[7] * B3[1 : GY + 1]
    wrap_rows(V3A)
    whole_sweep(THREE, V3A, V3B, B3, K3)

    def residual(g, v, s):
        r = B3[pl.ds(g + 1, CH)] + s - K3[6, pl.ds(g, CH)] * v
        B4[pl.ds(g + 1, CH)] = coarsen_lanes(r) * 0.125

    whole_sum(THREE, V3B, K3, residual)

    b4 = B4[1 : GY + 1]
    b4 = b4 - jnp.sum(jnp.sum(b4, axis=0), keepdims=True) * (1.0 / (GY * GX * 128))
    B4[1 : GY + 1] = b4
    V4A[1 : GY + 1] = K4[7] * b4
    wrap_rows(V4A)
    here, there = V4A, V4B
    for _ in range(7):
        whole_sweep(FOUR, here, there, B4, K4)
        here, there = there, here

    V3B[...] = V3B[...] + here[...]
    whole_sweep(THREE, V3B, V3A, B3, K3)
    whole_sweep(THREE, V3A, V3B, B3, K3)

    near = [
        pltpu.roll(V3B[lax.rem(gy + j - 1 + GY, GY) + 1], lax.rem(1 - gx + GX, GX), 0) for j in range(3)
    ]
    u = mm(jnp.concatenate(near, axis=0), MP3[...])
    for copy in h2:
        copy.wait_recv()
    pair = lax.broadcasted_iota(jnp.int32, (16, 128), 0) // 2
    for x3 in range(6):
        i, dx = x3 // 2, x3 % 2
        rise = jnp.zeros((16, 128), F32)
        for y3 in range(6):
            j, g = y3 // 2, 2 * dx + y3 % 2
            rise = jnp.where(pair == y3, u[8 * j + i : 8 * j + i + 1, 128 * g : 128 * g + 128], rise)
        for x in (2 * x3, 2 * x3 + 1):
            VA2[x] = V2H[x] + rise
    two = (B2H, CX2, CY2, CZ2)
    sweep(VA2, R2, *two, W2, 1, 11, True)
    sweep(R2, VA2, *two, W2, 2, 10, True)

    for k in range(8):
        rows = VA2[2 + k, 0:12, :]
        TP1[k, pl.ds(0, 12, stride=2), :] = rows
        TP1[k, pl.ds(1, 12, stride=2), :] = rows
    TR[0:8] = mm(TP1[...].reshape(8 * 24, 128), MP2[...]).reshape(8, 24, 128)
    for x in range(5, 19):
        VA1[x] = VB1[x] + TR[x // 2 - 2]
    sweep(VA1, R1, *one, W1, 6, 18, 2)
    sweep(R1, VA1, *one, W1, 7, 17, 2)

    for k in range(10):
        rows = VA1[7 + k, 7:17, :]
        TP0[k, pl.ds(2, 10, stride=2), :] = rows
        TP0[k, pl.ds(3, 10, stride=2), :] = rows
    u = mm(TP0[...].reshape(10 * 24, 128), MP1[...])
    for h in range(2):
        PE0[:, h] = u[:, 128 * h : 128 * h + 128].reshape(10, 24, 128)
    for copy in h0:
        copy.wait_recv()
    row = lax.broadcasted_iota(jnp.int32, (24, 128), 0)
    outer = (row == 2) | (row == 21)

    def raise_slab(x, carry):
        for h in range(2):
            VA0[x, h] = jnp.where(outer, VH[x, h], VB0[x, h]) + PE0[lax.div(x - 1, 2), h]
        return carry

    lax.fori_loop(2, 20, raise_slab, 0, unroll=2)
    for x in (1, 20):
        for h in range(2):
            VA0[x, h] = VH[x, h] + PE0[(x - 1) // 2, h]
    for copy in e0c + e0v + e0b:
        copy.wait_send()
    sweep(VA0, V0, *zero, W0, 2, 20, 2)

    def last(x, v, r):
        s = add(v, mul(get(W0, x), r))
        for h in range(2):
            out_ref[x - 3, :, 128 * h : 128 * h + 128] = s[h][4:20]

    flux_loop(V0, *zero, 3, 19, last, 2)

    for copy in c1 + b1 + h0 + h2:
        copy.wait_send()
    sent(C3, cas, car, cbs, cbr)
    sent(B3, bas, bar, bbs, bbr)


def solution(mesh):
    def vmem(*shape):
        return pltpu.VMEM(shape, F32)

    def half(*shape):
        return pltpu.VMEM(shape, BF16)

    dma = pltpu.SemaphoreType.DMA
    scratch = (
        [vmem(22, 2, 24, 128)] * 10
        + [vmem(8, 24, 128), vmem(10, 2, 24, 128), vmem(10, 24, 128)]
        + [vmem(24, 24, 128)] * 9
        + [vmem(8, 24, 128)]
        + [vmem(12, 16, 128)] * 11
        + [vmem(GY + 2, GX, 128)] * 4
        + [vmem(8, GY, GX, 128)]
        + [vmem(GY + 2, GX, 128)] * 4
        + [vmem(8, GY, GX, 128)]
        + [half(384, 128), half(128, 128), half(128, 256), half(128, 128), half(128, 512)]
        + [dma((6,)), dma((3, 8)), dma((3, 8))]
        + [dma((8,))] * 4
        + [dma((4,))] * 2
        + [dma((2, 8))] * 2
        + [dma((GX * NYC,)), dma((GX * NYC,)), dma((NZC,)), dma((NZC,))] * 2
    )

    def step(source, conductivity, guess):
        return pl.pallas_call(
            kernel,
            out_shape=jax.ShapeDtypeStruct(source.shape, F32),
            in_specs=[pl.BlockSpec(memory_space=pl.ANY)] * 3,
            out_specs=pl.BlockSpec(memory_space=pltpu.VMEM),
            scratch_shapes=scratch,
            compiler_params=pltpu.CompilerParams(
                collective_id=0, has_side_effects=True, vmem_limit_bytes=40 * 2**20
            ),
            name="vcycle",
        )(source, conductivity, guess)

    spec = P("gx", "gy", None)
    return jax.shard_map(step, mesh=mesh, in_specs=(spec, spec, spec), out_specs=spec, check_vma=False)
```

profile of v0, /device:TPU:1, one launch (start us, length us, event | category | flops | bytes accessed | tf_op | source)
XLA Modules:
  0.0 59.9 jit_solution(13250181220350596053)
XLA Ops:
  0.0 0.0 copy-start
  0.0 0.9 %copy-done = f32[16,16,256]{2,1,0:T(8,128)S(1)} copy-done((f32[16,16,256]{2,1,0:T(8,128)S(1)}, f32[16,16,256]{2,1,0:T(8,128)}, u32[]{:S(2)}) %copy-start) | copy-done | bytes 262168
  1.0 0.0 copy-start.1
  1.0 0.9 %copy-done.1 = f32[16,16,256]{2,1,0:T(8,128)S(1)} copy-done((f32[16,16,256]{2,1,0:T(8,128)S(1)}, f32[16,16,256]{2,1,0:T(8,128)}, u32[]{:S(2)}) %copy-start.1) | copy-done | bytes 262168
  1.9 0.0 copy-start.2
  1.9 0.9 %copy-done.2 = f32[16,16,256]{2,1,0:T(8,128)S(1)} copy-done((f32[16,16,256]{2,1,0:T(8,128)S(1)}, f32[16,16,256]{2,1,0:T(8,128)}, u32[]{:S(2)}) %copy-start.2) | copy-done | bytes 262168
  2.9 56.3 %vcycle.1 = f32[16,16,256]{2,1,0:T(8,128)S(1)} custom-call(f32[16,16,256]{2,1,0:T(8,128)S(1)} %copy-done, f32[16,16,256]{2,1,0:T(8,128)S(1)} %copy-done.1, f32[16,16,256]{2,1,0:T(8,128)S(1)} %copy-done.2), custom_call_target="tpu_custom_call" | custom-call | tf_op jit(solution)/shard_map/vcycle/pallas_call | solution.py:590
  59.2 0.7 %copy.5 = f32[16,16,256]{2,1,0:T(8,128)} copy(f32[16,16,256]{2,1,0:T(8,128)S(1)} %vcycle.1) | data formatting | bytes 524288
Async XLA Ops:
  0.0 0.9 %copy-start = (f32[16,16,256]{2,1,0:T(8,128)S(1)}, f32[16,16,256]{2,1,0:T(8,128)}, u32[]{:S(2)}) copy-start(f32[16,16,256]{2,1,0:T(8,128)} %src_ref.1) | copy-start | bytes 786436
  1.0 0.9 %copy-start.1 = (f32[16,16,256]{2,1,0:T(8,128)S(1)}, f32[16,16,256]{2,1,0:T(8,128)}, u32[]{:S(2)}) copy-start(f32[16,16,256]{2,1,0:T(8,128)} %cond_ref.1) | copy-start | bytes 786436
  1.9 0.9 %copy-start.2 = (f32[16,16,256]{2,1,0:T(8,128)S(1)}, f32[16,16,256]{2,1,0:T(8,128)}, u32[]{:S(2)}) copy-start(f32[16,16,256]{2,1,0:T(8,128)} %guess_ref.1) | copy-start | bytes 786436
where the time goes:
time: 60.1 us; the launch traced here: 59.9 us
  Pallas kernels  56.3 us (94%)
  local copies, waits for them, and re-layouts  3.55 us (6%)
    pallas_call x1, Pallas kernels, step(): pl.pallas_call(kernel, out_shape=jax.ShapeDtypeStruct(source.shape, F32),...  56.3 us
    unnamed x7, local copies, waits for them, and re-layouts  3.55 us

commit v1 on v0

--- a/solution.py
+++ b/solution.py
@@ -172,7 +172,8 @@
 
 THREE = (three_xp, three_xm, three_y, three_zp, three_zm)
 FOUR = (four_xp, four_xm, four_y, four_zp, four_zm)
-CH = 4
+CH = 16
+UN = 8
 
 
 def wrap_rows(ref):
@@ -236,8 +237,8 @@
     C1, CX1, CY1, CZ1, W1, B1, VA1, VB1, R1, TP1,
     C2, CX2, CY2, CZ2, W2, B2, VA2, VB2, R2, B2H, V2H,
     C3, B3, V3A, V3B, K3, C4, B4, V4A, V4B, K4,
-    MR, M3, MP1, MP2, MP3,
-    lsem, e0s, e0r, c1s, c1r, b1s, b1r, h0s, h0r, h2s, h2r, cas, car, cbs, cbr, bas, bar, bbs, bbr,
+    MR, M3, MP1, MP2, MP3, ROWS,
+    lsem, e0s, e0r, c1s, c1r, b1s, b1r, h0s, h0r, h2s, h2r, cg, bg,
 ):
     gx, gy = lax.axis_index("gx"), lax.axis_index("gy")
     yc, zc = lax.rem(gy, NYC), lax.div(gy, NYC)
@@ -284,18 +285,6 @@
     lax.fori_loop(1, GX * NYC, greet_plane, 0)
     lax.fori_loop(1, NZC, greet_z, 0)
 
-    def matrix(rows, columns, rule):
-        r = lax.broadcasted_iota(jnp.int32, (rows, columns), 0)
-        c = lax.broadcasted_iota(jnp.int32, (rows, columns), 1)
-        return jnp.where(rule(r, c), 1.0, 0.0).astype(BF16)
-
-    MR[0:256] = matrix(256, 128, lambda r, c: r // 2 == c)
-    MR[256:384] = matrix(128, 128, lambda r, c: r // 2 == c % 64)
-    M3[...] = matrix(128, 128, lambda r, c: (r < 64) & (r // 2 == c % 32))
-    MP1[...] = matrix(128, 256, lambda r, c: r == c // 2)
-    MP2[...] = matrix(128, 128, lambda r, c: r == c // 2)
-    MP3[...] = matrix(128, 512, lambda r, c: (r // 32 == c // 128) & (r % 32 == (c % 64) // 2))
-
     for copy in loads:
         copy.wait()
     pl.semaphore_wait(barrier, len(EIGHT) + GX * NYC - 1 + NZC - 1)
@@ -316,15 +305,31 @@
             src, dst = ref.at[pl.ds(sx, nx), pl.ds(sy, ny), :], ref.at[pl.ds(tx, nx), pl.ds(ty, ny), :]
         return remote(src, dst, send, recv, beside(*step))
 
-    def exchange(ref, base, extent, width, send, recv):
-        return [block_copy(ref, base, extent, o, width, send.at[i], recv.at[i]) for i, o in enumerate(EIGHT)]
+    def exchange(ref, base, extent, width, send, recv, corner=None):
+        return [
+            block_copy(ref, base, extent, o, corner if corner and o[0] and o[1] else width, send.at[i], recv.at[i])
+            for i, o in enumerate(EIGHT)
+        ]
 
     e0c = exchange(C0, (3, 4), 16, 3, e0s.at[0], e0r.at[0])
     e0v = exchange(V0, (3, 4), 16, 3, e0s.at[1], e0r.at[1])
     e0b = exchange(B0, (3, 4), 16, 2, e0s.at[2], e0r.at[2])
-    for copies in (e0c, e0v, e0b):
-        for copy in copies:
-            copy.start()
+    for faces in ((0, 1), (2, 3, 4, 5), (6, 7)):
+        for copies in (e0c, e0v, e0b):
+            for i in faces:
+                copies[i].start()
+
+    def matrix(rows, columns, rule):
+        r = lax.broadcasted_iota(jnp.int32, (rows, columns), 0)
+        c = lax.broadcasted_iota(jnp.int32, (rows, columns), 1)
+        return jnp.where(rule(r, c), 1.0, 0.0).astype(BF16)
+
+    MR[0:256] = matrix(256, 128, lambda r, c: r // 2 == c)
+    MR[256:384] = matrix(128, 128, lambda r, c: r // 2 == c % 64)
+    M3[...] = matrix(128, 128, lambda r, c: (r < 64) & (r // 2 == c % 32))
+    MP1[...] = matrix(128, 256, lambda r, c: r == c // 2)
+    MP2[...] = matrix(128, 128, lambda r, c: r == c // 2)
+    MP3[...] = matrix(128, 512, lambda r, c: (r // 32 == c // 128) & (r % 32 == (c % 64) // 2))
 
     def restrict_zero(ref, scale):
         pairs = [
@@ -350,44 +355,38 @@
             row = jnp.where(group == g, s[at : at + 1] + s[at + 1 : at + 2], row)
         return row
 
-    def plane_copy(ref, k, send, recv):
+    def plane_copy(ref, k, sems):
         part = ref.at[gy + 1, pl.ds(gx, 1), :]
-        return remote(part, part, send.at[k], recv.at[k], in_plane(k))
-
-    def z_copy(ref, k, send, recv):
+        return remote(part, part, sems.at[0], sems.at[1], in_plane(k))
+
+    def z_copy(ref, k, sems):
         part = ref.at[pl.ds(zc * NYC + 1, NYC)]
-        return remote(part, part, send.at[k], recv.at[k], along_z(k))
-
-    def start_plane(ref, send, recv):
+        return remote(part, part, sems.at[2], sems.at[3], along_z(k))
+
+    def start_plane(ref, sems):
         def go(k, carry):
-            plane_copy(ref, k, send, recv).start()
+            plane_copy(ref, k, sems).start()
             return carry
 
-        lax.fori_loop(1, GX * NYC, go, 0)
-
-    def landed_plane(ref, send, recv):
-        def go(k, carry):
-            plane_copy(ref, k, send, recv).wait_recv()
-            return carry
-
-        lax.fori_loop(1, GX * NYC, go, 0)
-
-    def start_z(ref, send, recv):
+        lax.fori_loop(1, GX * NYC, go, 0, unroll=True)
+
+    def start_z(ref, sems):
         for k in range(1, NZC):
-            z_copy(ref, k, send, recv).start()
-
-    def landed_z(ref, send, recv):
-        for k in range(1, NZC):
-            z_copy(ref, k, send, recv).wait_recv()
-
-    def sent(ref, plane_send, plane_recv, z_send, z_recv):
-        def go(k, carry):
-            plane_copy(ref, k, plane_send, plane_recv).wait_send()
-            return carry
-
-        lax.fori_loop(1, GX * NYC, go, 0)
-        for k in range(1, NZC):
-            z_copy(ref, k, z_send, z_recv).wait_send()
+            z_copy(ref, k, sems).start()
+
+    def all_bytes(ref, kind, sem):
+        part = ROWS if kind == 0 else ref.at[pl.ds(1, GY - NYC)]
+        pltpu.make_async_copy(part, part, sem).wait()
+
+    def landed_plane(ref, sems):
+        all_bytes(ref, 0, sems.at[1])
+
+    def landed_z(ref, sems):
+        all_bytes(ref, 1, sems.at[3])
+
+    def sent(ref, sems):
+        all_bytes(ref, 0, sems.at[0])
+        all_bytes(ref, 1, sems.at[2])
 
     C1[8:16, 8:16] = restrict_zero(C0, 0.125 * 0.25)
     c1 = exchange(C1, (8, 8), 8, 8, c1s, c1r)
@@ -395,19 +394,19 @@
         copy.start()
     C2[4:8, 4:8] = restrict_one(C1, 8, 4, 8, 8, 0.125 * 0.25)
     C3[gy + 1, pl.ds(gx, 1), :] = restrict_two(C2, 0.125 * 0.25)
-    start_plane(C3, cas, car)
+    start_plane(C3, cg)
 
     for copy in e0c:
         copy.wait_recv()
-    coefficients(C0, CX0, CY0, CZ0, W0, 22, 2)
+    coefficients(C0, CX0, CY0, CZ0, W0, 22, UN)
     for copy in e0v + e0b:
         copy.wait_recv()
     zero = (B0, CX0, CY0, CZ0)
-    sweep(V0, VA0, *zero, W0, 1, 21, 2)
-    sweep(VA0, VB0, *zero, W0, 2, 20, 2)
-    flux_loop(VB0, *zero, 3, 19, lambda x, v, r: put(VA0, x, r), 2)
+    sweep(V0, VA0, *zero, W0, 1, 21, UN)
+    sweep(VA0, VB0, *zero, W0, 2, 20, UN)
+    flux_loop(VB0, *zero, 3, 19, lambda x, v, r: put(VA0, x, r), UN)
     B1[8:16, 8:16] = restrict_zero(VA0, 0.125)
-    b1 = exchange(B1, (8, 8), 8, 8, b1s, b1r)
+    b1 = exchange(B1, (8, 8), 8, 6, b1s, b1r, 5)
     for copy in b1:
         copy.start()
 
@@ -424,12 +423,12 @@
     for copy in h0:
         copy.start()
 
-    landed_plane(C3, cas, car)
-    start_z(C3, cbs, cbr)
+    landed_plane(C3, cg)
+    start_z(C3, cg)
 
     for copy in c1:
         copy.wait_recv()
-    coefficients(C1, CX1, CY1, CZ1, W1, 24, 2)
+    coefficients(C1, CX1, CY1, CZ1, W1, 24, UN)
     for k in range(3):
         C2[4 * k : 4 * k + 4, 0:12] = restrict_one(C1, 8 * k, 4, 0, 24, 0.125 * 0.25)
     coefficients(C2, CX2, CY2, CZ2, W2, 12, True)
@@ -442,8 +441,8 @@
 
     one = (B1, CX1, CY1, CZ1)
     from_zero(VA1, B1, W1, 2, 22)
-    sweep(VA1, VB1, *one, W1, 3, 21, 2)
-    flux_loop(VB1, *one, 4, 20, lambda x, v, r: put(R1, x, r), 2)
+    sweep(VA1, VB1, *one, W1, 3, 21, UN)
+    flux_loop(VB1, *one, 4, 20, lambda x, v, r: put(R1, x, r), UN)
     B2[2:10, 0:12] = restrict_one(R1, 4, 8, 0, 24, 0.125)
 
     two = (B2, CX2, CY2, CZ2)
@@ -451,23 +450,23 @@
     sweep(VA2, VB2, *two, W2, 3, 9, True)
     flux_loop(VB2, *two, 4, 8, lambda x, v, r: put(R2, x, r), True)
     B3[gy + 1, pl.ds(gx, 1), :] = restrict_two(R2, 0.125)
-    start_plane(B3, bas, bar)
+    start_plane(B3, bg)
     B2H[4:8, 4:8] = B2[4:8, 4:8]
     V2H[4:8, 4:8] = VB2[4:8, 4:8]
     h2 = exchange(B2H, (4, 4), 4, 4, h2s.at[0], h2r.at[0]) + exchange(V2H, (4, 4), 4, 4, h2s.at[1], h2r.at[1])
     for copy in h2:
         copy.start()
 
-    landed_z(C3, cbs, cbr)
+    landed_z(C3, cg)
     wrap_rows(C3)
     whole_coefficients(THREE, C3, K3)
     C4[1 : GY + 1] = coarsen_lanes(C3[1 : GY + 1]) * (0.125 * 0.25)
     wrap_rows(C4)
     whole_coefficients(FOUR, C4, K4)
 
-    landed_plane(B3, bas, bar)
-    start_z(B3, bbs, bbr)
-    landed_z(B3, bbs, bbr)
+    landed_plane(B3, bg)
+    start_z(B3, bg)
+    landed_z(B3, bg)
 
     V3A[1 : GY + 1] = K3[7] * B3[1 : GY + 1]
     wrap_rows(V3A)
@@ -519,8 +518,8 @@
     TR[0:8] = mm(TP1[...].reshape(8 * 24, 128), MP2[...]).reshape(8, 24, 128)
     for x in range(5, 19):
         VA1[x] = VB1[x] + TR[x // 2 - 2]
-    sweep(VA1, R1, *one, W1, 6, 18, 2)
-    sweep(R1, VA1, *one, W1, 7, 17, 2)
+    sweep(VA1, R1, *one, W1, 6, 18, UN)
+    sweep(R1, VA1, *one, W1, 7, 17, UN)
 
     for k in range(10):
         rows = VA1[7 + k, 7:17, :]
@@ -539,25 +538,25 @@
             VA0[x, h] = jnp.where(outer, VH[x, h], VB0[x, h]) + PE0[lax.div(x - 1, 2), h]
         return carry
 
-    lax.fori_loop(2, 20, raise_slab, 0, unroll=2)
+    lax.fori_loop(2, 20, raise_slab, 0, unroll=UN)
     for x in (1, 20):
         for h in range(2):
             VA0[x, h] = VH[x, h] + PE0[(x - 1) // 2, h]
     for copy in e0c + e0v + e0b:
         copy.wait_send()
-    sweep(VA0, V0, *zero, W0, 2, 20, 2)
+    sweep(VA0, V0, *zero, W0, 2, 20, UN)
 
     def last(x, v, r):
         s = add(v, mul(get(W0, x), r))
         for h in range(2):
             out_ref[x - 3, :, 128 * h : 128 * h + 128] = s[h][4:20]
 
-    flux_loop(V0, *zero, 3, 19, last, 2)
+    flux_loop(V0, *zero, 3, 19, last, UN)
 
     for copy in c1 + b1 + h0 + h2:
         copy.wait_send()
-    sent(C3, cas, car, cbs, cbr)
-    sent(B3, bas, bar, bbs, bbr)
+    sent(C3, cg)
+    sent(B3, bg)
 
 
 def solution(mesh):
@@ -579,11 +578,12 @@
         + [vmem(GY + 2, GX, 128)] * 4
         + [vmem(8, GY, GX, 128)]
         + [half(384, 128), half(128, 128), half(128, 256), half(128, 128), half(128, 512)]
+        + [vmem(GX * NYC - 1, 128)]
         + [dma((6,)), dma((3, 8)), dma((3, 8))]
         + [dma((8,))] * 4
         + [dma((4,))] * 2
         + [dma((2, 8))] * 2
-        + [dma((GX * NYC,)), dma((GX * NYC,)), dma((NZC,)), dma((NZC,))] * 2
+        + [dma((4,))] * 2
     )
 
     def step(source, conductivity, guess):
@@ -594,7 +594,7 @@
             out_specs=pl.BlockSpec(memory_space=pltpu.VMEM),
             scratch_shapes=scratch,
             compiler_params=pltpu.CompilerParams(
-                collective_id=0, has_side_effects=True, vmem_limit_bytes=40 * 2**20
+                collective_id=0, has_side_effects=True, vmem_limit_bytes=54848 * 2**10
             ),
             name="vcycle",
         )(source, conductivity, guess)

time: 60.1 us -> 46.6 us (0.78)
  Pallas kernels: 56.3 us -> 45.8 us
  local copies, waits for them, and re-layouts: 3.55 us -> 0.71 us
    pallas_call x1, Pallas kernels: 56.3 us -> 45.8 us  [step(): pl.pallas_call(kernel, out_shape=jax.ShapeDtypeStruct(source.shape, F32),...]
    unnamed x7 -> x1, local copies, waits for them, and re-layouts: 3.55 us -> 0.71 us
where the time goes in v1:
time: 46.6 us; the launch traced here: 46.5 us
  Pallas kernels  45.8 us (98%)
  local copies, waits for them, and re-layouts  0.71 us (2%)
    pallas_call x1, Pallas kernels, step(): pl.pallas_call(kernel, out_shape=jax.ShapeDtypeStruct(source.shape, F32),...  45.8 us

profile of v1, /device:TPU:1, one launch (start us, length us, event | category | flops | bytes accessed | tf_op | source)
XLA Modules:
  0.0 46.5 jit_solution(16537984730299874144)
XLA Ops:
  0.0 45.8 %vcycle.1 = f32[16,16,256]{2,1,0:T(8,128)S(1)} custom-call(f32[16,16,256]{2,1,0:T(8,128)} %src_ref.1, f32[16,16,256]{2,1,0:T(8,128)} %cond_ref.1, f32[16,16,256]{2,1,0:T(8,128)} %guess_ref.1), custom_call_target="tpu_custom_call" | custom-call | tf_op jit(solution)/shard_map/vcycle/pallas_call | solution.py:590
  45.8 0.7 %copy.5 = f32[16,16,256]{2,1,0:T(8,128)} copy(f32[16,16,256]{2,1,0:T(8,128)S(1)} %vcycle.1) | data formatting | bytes 524288

commit v2 on v1

--- a/solution.py
+++ b/solution.py
@@ -9,6 +9,10 @@
 F32, BF16 = jnp.float32, jnp.bfloat16
 OMEGA = 0.8
 GX, GY, NYC, NZC = 8, 32, 4, 8
+FAR_FIRST = sorted(
+    ((dx, dy) for dx in range(GX) for dy in range(NYC) if dx or dy),
+    key=lambda o: -(min(o[0], GX - o[0]) + 2 * min(o[1], NYC - o[1])),
+)
 EIGHT = [(0, 1), (0, -1), (1, 1), (1, -1), (-1, 1), (-1, -1), (1, 0), (-1, 0)]
 
 
@@ -76,7 +80,11 @@
     return each(lambda p, q: p * q, a, b)
 
 
-def coefficients(c_ref, cx_ref, cy_ref, cz_ref, w_ref, slabs, unroll):
+def steps_of(count, most):
+    return max(n for n in range(1, most + 1) if count % n == 0)
+
+
+def coefficients(c_ref, cx_ref, cy_ref, cz_ref, w_ref, slabs):
     c = get(c_ref, 0)
     n = get(c_ref, 1)
     first = each(harmonic, c, n)
@@ -95,10 +103,10 @@
         put(w_ref, x, each(lambda p: OMEGA / p, d))
         return n, ex
 
-    lax.fori_loop(1, slabs - 1, body, (n, first), unroll=unroll)
-
-
-def flux_loop(v_ref, b_ref, cx_ref, cy_ref, cz_ref, lo, hi, emit, unroll):
+    lax.fori_loop(1, slabs - 1, body, (n, first), unroll=steps_of(slabs - 2, UNROLL_FACES[len(c_ref.shape)]))
+
+
+def flux_loop(v_ref, b_ref, cx_ref, cy_ref, cz_ref, lo, hi, emit):
     v = get(v_ref, lo)
     before = mul(get(cx_ref, lo - 1), sub(v, get(v_ref, lo - 1)))
 
@@ -112,14 +120,14 @@
         emit(x, v, add(get(b_ref, x), r))
         return n, tx
 
-    lax.fori_loop(lo, hi, body, (v, before), unroll=unroll)
-
-
-def sweep(v_ref, to_ref, b_ref, cx_ref, cy_ref, cz_ref, w_ref, lo, hi, unroll):
+    lax.fori_loop(lo, hi, body, (v, before), unroll=steps_of(hi - lo, UNROLL[len(v_ref.shape)]))
+
+
+def sweep(v_ref, to_ref, b_ref, cx_ref, cy_ref, cz_ref, w_ref, lo, hi):
     def emit(x, v, r):
         put(to_ref, x, add(v, mul(get(w_ref, x), r)))
 
-    flux_loop(v_ref, b_ref, cx_ref, cy_ref, cz_ref, lo, hi, emit, unroll)
+    flux_loop(v_ref, b_ref, cx_ref, cy_ref, cz_ref, lo, hi, emit)
 
 
 def lane(shape):
@@ -172,8 +180,8 @@
 
 THREE = (three_xp, three_xm, three_y, three_zp, three_zm)
 FOUR = (four_xp, four_xm, four_y, four_zp, four_zm)
-CH = 16
-UN = 8
+UNROLL = {4: 10, 3: 20}
+UNROLL_FACES = {4: 10, 3: 11}
 
 
 def wrap_rows(ref):
@@ -181,12 +189,16 @@
     ref[GY + 1] = ref[1]
 
 
+def chunks(lo, hi):
+    parts = -(-(hi - lo) // 16)
+    cuts = [lo + (hi - lo) * i // parts for i in range(parts + 1)]
+    return list(zip(cuts[:-1], cuts[1:]))
+
+
 def whole_coefficients(level, c_ref, k_ref):
     xp, xm, y, zplus, zminus = level
-
-    def body(i, carry):
-        g = i * CH
-        ext = c_ref[pl.ds(g, CH + 2)]
+    for lo, hi in chunks(0, GY):
+        ext = c_ref[lo : hi + 2]
         c = ext[1:-1]
         up, down = y(ext)
         ex = harmonic(c, xp(c))
@@ -195,34 +207,27 @@
         wx, wz = xm(ex), zminus(ez)
         d = (ex + wx) + (ey + wy) + (ez + wz)
         for j, value in enumerate((ex, wx, ey, wy, ez, wz, d, OMEGA / d)):
-            k_ref[j, pl.ds(g, CH)] = value
-        return carry
-
-    lax.fori_loop(0, GY // CH, body, 0, unroll=True)
-
-
-def whole_sum(level, v_ref, k_ref, emit):
+            k_ref[j, lo:hi] = value
+
+
+def whole_sum(level, v_ref, k_ref, emit, first, last):
     xp, xm, y, zplus, zminus = level
-
-    def body(i, carry):
-        g = i * CH
-        ext = v_ref[pl.ds(g, CH + 2)]
+    for lo, hi in chunks(first, last):
+        ext = v_ref[lo : hi + 2]
         v = ext[1:-1]
         up, down = y(ext)
-        k = [k_ref[j, pl.ds(g, CH)] for j in range(6)]
+        k = [k_ref[j, lo:hi] for j in range(6)]
         s = (k[0] * xp(v) + k[1] * xm(v)) + (k[2] * up + k[3] * down)
-        emit(g, v, s + (k[4] * zplus(v) + k[5] * zminus(v)))
-        return carry
-
-    lax.fori_loop(0, GY // CH, body, 0, unroll=True)
-
-
-def whole_sweep(level, v_ref, to_ref, b_ref, k_ref):
-    def emit(g, v, s):
-        to_ref[pl.ds(g + 1, CH)] = (1.0 - OMEGA) * v + k_ref[7, pl.ds(g, CH)] * (b_ref[pl.ds(g + 1, CH)] + s)
-
-    whole_sum(level, v_ref, k_ref, emit)
-    wrap_rows(to_ref)
+        emit(lo, hi, v, s + (k[4] * zplus(v) + k[5] * zminus(v)))
+
+
+def whole_sweep(level, v_ref, to_ref, b_ref, k_ref, first=0, last=GY):
+    def emit(lo, hi, v, s):
+        to_ref[lo + 1 : hi + 1] = (1.0 - OMEGA) * v + k_ref[7, lo:hi] * (b_ref[lo + 1 : hi + 1] + s)
+
+    whole_sum(level, v_ref, k_ref, emit, first, last)
+    if last - first == GY:
+        wrap_rows(to_ref)
 
 
 def coarsen_lanes(v):
@@ -236,7 +241,7 @@
     V0, B0, C0, CX0, CY0, CZ0, W0, VA0, VB0, VH, TR, PE0, TP0,
     C1, CX1, CY1, CZ1, W1, B1, VA1, VB1, R1, TP1,
     C2, CX2, CY2, CZ2, W2, B2, VA2, VB2, R2, B2H, V2H,
-    C3, B3, V3A, V3B, K3, C4, B4, V4A, V4B, K4,
+    C3, B3, V3A, V3B, K3, C4, B4, V4A, V4B, K4, GC, GB,
     MR, M3, MP1, MP2, MP3, ROWS,
     lsem, e0s, e0r, c1s, c1r, b1s, b1r, h0s, h0r, h2s, h2r, cg, bg,
 ):
@@ -285,8 +290,6 @@
     lax.fori_loop(1, GX * NYC, greet_plane, 0)
     lax.fori_loop(1, NZC, greet_z, 0)
 
-    for copy in loads:
-        copy.wait()
     pl.semaphore_wait(barrier, len(EIGHT) + GX * NYC - 1 + NZC - 1)
 
     def edge(base, extent, step, width):
@@ -311,11 +314,14 @@
             for i, o in enumerate(EIGHT)
         ]
 
-    e0c = exchange(C0, (3, 4), 16, 3, e0s.at[0], e0r.at[0])
-    e0v = exchange(V0, (3, 4), 16, 3, e0s.at[1], e0r.at[1])
-    e0b = exchange(B0, (3, 4), 16, 2, e0s.at[2], e0r.at[2])
+    e0c = exchange(C0, (3, 4), 16, 3, e0s.at[0], e0r.at[0], 2)
+    e0v = exchange(V0, (3, 4), 16, 3, e0s.at[1], e0r.at[1], 2)
+    e0b = exchange(B0, (3, 4), 16, 2, e0s.at[2], e0r.at[2], 1)
     for faces in ((0, 1), (2, 3, 4, 5), (6, 7)):
-        for copies in (e0c, e0v, e0b):
+        for n, copies in enumerate((e0c, e0v, e0b)):
+            if faces[0] == 0:
+                loads[2 * n].wait()
+                loads[2 * n + 1].wait()
             for i in faces:
                 copies[i].start()
 
@@ -355,56 +361,54 @@
             row = jnp.where(group == g, s[at : at + 1] + s[at + 1 : at + 2], row)
         return row
 
-    def plane_copy(ref, k, sems):
-        part = ref.at[gy + 1, pl.ds(gx, 1), :]
-        return remote(part, part, sems.at[0], sems.at[1], in_plane(k))
-
     def z_copy(ref, k, sems):
-        part = ref.at[pl.ds(zc * NYC + 1, NYC)]
-        return remote(part, part, sems.at[2], sems.at[3], along_z(k))
+        src = ref.at[NZC // 2, yc, pl.ds(gx, 1), :]
+        dst = ref.at[(NZC // 2 - k) % NZC, yc, pl.ds(gx, 1), :]
+        return remote(src, dst, sems.at[0], sems.at[1], along_z(k))
+
+    def plane_copy(ref, dx, dy, sems):
+        part = ref.at[:, yc, pl.ds(gx, 1), :]
+        return remote(part, part, sems.at[2], sems.at[3], in_plane(dx * NYC + dy))
+
+    def start_z(ref, sems):
+        for k in (4, 3, 5, 2, 6, 1, 7):
+            z_copy(ref, k, sems).start()
 
     def start_plane(ref, sems):
-        def go(k, carry):
-            plane_copy(ref, k, sems).start()
-            return carry
-
-        lax.fori_loop(1, GX * NYC, go, 0, unroll=True)
-
-    def start_z(ref, sems):
-        for k in range(1, NZC):
-            z_copy(ref, k, sems).start()
-
-    def all_bytes(ref, kind, sem):
-        part = ROWS if kind == 0 else ref.at[pl.ds(1, GY - NYC)]
+        for dx, dy in FAR_FIRST:
+            plane_copy(ref, dx, dy, sems).start()
+
+    def all_bytes(kind, sem):
+        part = ROWS.at[0, pl.ds(0, NZC - 1), :] if kind == 0 else ROWS
         pltpu.make_async_copy(part, part, sem).wait()
 
-    def landed_plane(ref, sems):
-        all_bytes(ref, 0, sems.at[1])
-
-    def landed_z(ref, sems):
-        all_bytes(ref, 1, sems.at[3])
-
-    def sent(ref, sems):
-        all_bytes(ref, 0, sems.at[0])
-        all_bytes(ref, 1, sems.at[2])
+    def landed_z(sems):
+        all_bytes(0, sems.at[1])
+
+    def landed_plane(sems):
+        all_bytes(1, sems.at[3])
+
+    def sent(sems):
+        all_bytes(0, sems.at[0])
+        all_bytes(1, sems.at[2])
 
     C1[8:16, 8:16] = restrict_zero(C0, 0.125 * 0.25)
     c1 = exchange(C1, (8, 8), 8, 8, c1s, c1r)
     for copy in c1:
         copy.start()
     C2[4:8, 4:8] = restrict_one(C1, 8, 4, 8, 8, 0.125 * 0.25)
-    C3[gy + 1, pl.ds(gx, 1), :] = restrict_two(C2, 0.125 * 0.25)
-    start_plane(C3, cg)
+    GC[NZC // 2, yc, pl.ds(gx, 1), :] = restrict_two(C2, 0.125 * 0.25)
+    start_z(GC, cg)
 
     for copy in e0c:
         copy.wait_recv()
-    coefficients(C0, CX0, CY0, CZ0, W0, 22, UN)
+    coefficients(C0, CX0, CY0, CZ0, W0, 22)
     for copy in e0v + e0b:
         copy.wait_recv()
     zero = (B0, CX0, CY0, CZ0)
-    sweep(V0, VA0, *zero, W0, 1, 21, UN)
-    sweep(VA0, VB0, *zero, W0, 2, 20, UN)
-    flux_loop(VB0, *zero, 3, 19, lambda x, v, r: put(VA0, x, r), UN)
+    sweep(V0, VA0, *zero, W0, 1, 21)
+    sweep(VA0, VB0, *zero, W0, 2, 20)
+    flux_loop(VB0, *zero, 3, 19, lambda x, v, r: put(VA0, x, r))
     B1[8:16, 8:16] = restrict_zero(VA0, 0.125)
     b1 = exchange(B1, (8, 8), 8, 6, b1s, b1r, 5)
     for copy in b1:
@@ -418,20 +422,24 @@
             ((0, -1), (3, 3, 16), (5, 21, 1)),
             ((1, 0), (17, 1, 1), (4, 4, 16)),
             ((-1, 0), (4, 20, 1), (4, 4, 16)),
+            ((1, 1), (18, 2, 1), (19, 3, 1)),
+            ((1, -1), (18, 2, 1), (4, 20, 1)),
+            ((-1, 1), (3, 19, 1), (19, 3, 1)),
+            ((-1, -1), (3, 19, 1), (4, 20, 1)),
         ))
     ]
     for copy in h0:
         copy.start()
 
-    landed_plane(C3, cg)
-    start_z(C3, cg)
+    landed_z(cg)
+    start_plane(GC, cg)
 
     for copy in c1:
         copy.wait_recv()
-    coefficients(C1, CX1, CY1, CZ1, W1, 24, UN)
+    coefficients(C1, CX1, CY1, CZ1, W1, 24)
     for k in range(3):
         C2[4 * k : 4 * k + 4, 0:12] = restrict_one(C1, 8 * k, 4, 0, 24, 0.125 * 0.25)
-    coefficients(C2, CX2, CY2, CZ2, W2, 12, True)
+    coefficients(C2, CX2, CY2, CZ2, W2, 12)
 
     for copy in b1:
         copy.wait_recv()
@@ -441,59 +449,61 @@
 
     one = (B1, CX1, CY1, CZ1)
     from_zero(VA1, B1, W1, 2, 22)
-    sweep(VA1, VB1, *one, W1, 3, 21, UN)
-    flux_loop(VB1, *one, 4, 20, lambda x, v, r: put(R1, x, r), UN)
+    sweep(VA1, VB1, *one, W1, 3, 21)
+    flux_loop(VB1, *one, 4, 20, lambda x, v, r: put(R1, x, r))
     B2[2:10, 0:12] = restrict_one(R1, 4, 8, 0, 24, 0.125)
 
     two = (B2, CX2, CY2, CZ2)
     from_zero(VA2, B2, W2, 2, 10)
-    sweep(VA2, VB2, *two, W2, 3, 9, True)
-    flux_loop(VB2, *two, 4, 8, lambda x, v, r: put(R2, x, r), True)
-    B3[gy + 1, pl.ds(gx, 1), :] = restrict_two(R2, 0.125)
-    start_plane(B3, bg)
+    sweep(VA2, VB2, *two, W2, 3, 9)
+    flux_loop(VB2, *two, 4, 8, lambda x, v, r: put(R2, x, r))
+    GB[NZC // 2, yc, pl.ds(gx, 1), :] = restrict_two(R2, 0.125)
+    start_z(GB, bg)
     B2H[4:8, 4:8] = B2[4:8, 4:8]
     V2H[4:8, 4:8] = VB2[4:8, 4:8]
     h2 = exchange(B2H, (4, 4), 4, 4, h2s.at[0], h2r.at[0]) + exchange(V2H, (4, 4), 4, 4, h2s.at[1], h2r.at[1])
     for copy in h2:
         copy.start()
 
-    landed_z(C3, cg)
+    landed_plane(cg)
+    C3[1 : GY + 1] = GC[...].reshape(GY, GX, 128)
     wrap_rows(C3)
     whole_coefficients(THREE, C3, K3)
     C4[1 : GY + 1] = coarsen_lanes(C3[1 : GY + 1]) * (0.125 * 0.25)
     wrap_rows(C4)
     whole_coefficients(FOUR, C4, K4)
 
-    landed_plane(B3, bg)
-    start_z(B3, bg)
-    landed_z(B3, bg)
-
-    V3A[1 : GY + 1] = K3[7] * B3[1 : GY + 1]
+    landed_z(bg)
+    start_plane(GB, bg)
+    landed_plane(bg)
+
+    b3 = GB[...].reshape(GY, GX, 128)
+    B3[1 : GY + 1] = b3
+    V3A[1 : GY + 1] = K3[7] * b3
     wrap_rows(V3A)
     whole_sweep(THREE, V3A, V3B, B3, K3)
 
-    def residual(g, v, s):
-        r = B3[pl.ds(g + 1, CH)] + s - K3[6, pl.ds(g, CH)] * v
-        B4[pl.ds(g + 1, CH)] = coarsen_lanes(r) * 0.125
-
-    whole_sum(THREE, V3B, K3, residual)
+    def residual(lo, hi, v, s):
+        r = B3[lo + 1 : hi + 1] + s - K3[6, lo:hi] * v
+        B4[lo + 1 : hi + 1] = coarsen_lanes(r) * 0.125
+
+    whole_sum(THREE, V3B, K3, residual, 0, GY)
 
     b4 = B4[1 : GY + 1]
     b4 = b4 - jnp.sum(jnp.sum(b4, axis=0), keepdims=True) * (1.0 / (GY * GX * 128))
     B4[1 : GY + 1] = b4
-    V4A[1 : GY + 1] = K4[7] * b4
-    wrap_rows(V4A)
+    V4A[7:31] = K4[7, 6:30] * b4[6:30]
     here, there = V4A, V4B
-    for _ in range(7):
-        whole_sweep(FOUR, here, there, B4, K4)
+    for i in range(7):
+        whole_sweep(FOUR, here, there, B4, K4, 7 + i, 29 - i)
         here, there = there, here
 
-    V3B[...] = V3B[...] + here[...]
-    whole_sweep(THREE, V3B, V3A, B3, K3)
-    whole_sweep(THREE, V3A, V3B, B3, K3)
+    V3B[14:24] = V3B[14:24] + here[14:24]
+    whole_sweep(THREE, V3B, V3A, B3, K3, 14, 22)
+    whole_sweep(THREE, V3A, V3B, B3, K3, 15, 21)
 
     near = [
-        pltpu.roll(V3B[lax.rem(gy + j - 1 + GY, GY) + 1], lax.rem(1 - gx + GX, GX), 0) for j in range(3)
+        pltpu.roll(V3B[4 * (NZC // 2) + yc + j], lax.rem(1 - gx + GX, GX), 0) for j in range(3)
     ]
     u = mm(jnp.concatenate(near, axis=0), MP3[...])
     for copy in h2:
@@ -508,8 +518,8 @@
         for x in (2 * x3, 2 * x3 + 1):
             VA2[x] = V2H[x] + rise
     two = (B2H, CX2, CY2, CZ2)
-    sweep(VA2, R2, *two, W2, 1, 11, True)
-    sweep(R2, VA2, *two, W2, 2, 10, True)
+    sweep(VA2, R2, *two, W2, 1, 11)
+    sweep(R2, VA2, *two, W2, 2, 10)
 
     for k in range(8):
         rows = VA2[2 + k, 0:12, :]
@@ -518,8 +528,8 @@
     TR[0:8] = mm(TP1[...].reshape(8 * 24, 128), MP2[...]).reshape(8, 24, 128)
     for x in range(5, 19):
         VA1[x] = VB1[x] + TR[x // 2 - 2]
-    sweep(VA1, R1, *one, W1, 6, 18, UN)
-    sweep(R1, VA1, *one, W1, 7, 17, UN)
+    sweep(VA1, R1, *one, W1, 6, 18)
+    sweep(R1, VA1, *one, W1, 7, 17)
 
     for k in range(10):
         rows = VA1[7 + k, 7:17, :]
@@ -538,25 +548,28 @@
             VA0[x, h] = jnp.where(outer, VH[x, h], VB0[x, h]) + PE0[lax.div(x - 1, 2), h]
         return carry
 
-    lax.fori_loop(2, 20, raise_slab, 0, unroll=UN)
-    for x in (1, 20):
-        for h in range(2):
+    lax.fori_loop(3, 19, raise_slab, 0, unroll=8)
+    corner = (row == 3) | (row == 20)
+    for h in range(2):
+        for x in (1, 20):
             VA0[x, h] = VH[x, h] + PE0[(x - 1) // 2, h]
+        for x in (2, 19):
+            VA0[x, h] = jnp.where(corner, VH[x, h], VB0[x, h]) + PE0[(x - 1) // 2, h]
     for copy in e0c + e0v + e0b:
         copy.wait_send()
-    sweep(VA0, V0, *zero, W0, 2, 20, UN)
+    sweep(VA0, V0, *zero, W0, 2, 20)
 
     def last(x, v, r):
         s = add(v, mul(get(W0, x), r))
         for h in range(2):
             out_ref[x - 3, :, 128 * h : 128 * h + 128] = s[h][4:20]
 
-    flux_loop(V0, *zero, 3, 19, last, UN)
+    flux_loop(V0, *zero, 3, 19, last)
 
     for copy in c1 + b1 + h0 + h2:
         copy.wait_send()
-    sent(C3, cg)
-    sent(B3, bg)
+    sent(cg)
+    sent(bg)
 
 
 def solution(mesh):
@@ -577,11 +590,11 @@
         + [vmem(8, GY, GX, 128)]
         + [vmem(GY + 2, GX, 128)] * 4
         + [vmem(8, GY, GX, 128)]
+        + [vmem(NZC, NYC, GX, 128)] * 2
         + [half(384, 128), half(128, 128), half(128, 256), half(128, 128), half(128, 512)]
-        + [vmem(GX * NYC - 1, 128)]
+        + [vmem(GX * NYC - 1, NZC, 128)]
         + [dma((6,)), dma((3, 8)), dma((3, 8))]
-        + [dma((8,))] * 4
-        + [dma((4,))] * 2
+        + [dma((8,))] * 6
         + [dma((2, 8))] * 2
         + [dma((4,))] * 2
     )

time: 46.6 us -> 41.5 us (0.89)
  Pallas kernels: 45.8 us -> 40.8 us
    pallas_call x1, Pallas kernels: 45.8 us -> 40.8 us  [step(): pl.pallas_call(kernel, out_shape=jax.ShapeDtypeStruct(source.shape, F32),...]
where the time goes in v2:
time: 41.5 us
  Pallas kernels  40.8 us (98%)
  local copies, waits for them, and re-layouts  0.71 us (2%)
    pallas_call x1, Pallas kernels, step(): pl.pallas_call(kernel, out_shape=jax.ShapeDtypeStruct(source.shape, F32),...  40.8 us

profile of v2, /device:TPU:1, one launch (start us, length us, event | category | flops | bytes accessed | tf_op | source)
XLA Modules:
  0.0 41.5 jit_solution(8731218936476419902)
XLA Ops:
  0.0 40.8 %vcycle.1 = f32[16,16,256]{2,1,0:T(8,128)S(1)} custom-call(f32[16,16,256]{2,1,0:T(8,128)} %src_ref.1, f32[16,16,256]{2,1,0:T(8,128)} %cond_ref.1, f32[16,16,256]{2,1,0:T(8,128)} %guess_ref.1), custom_call_target="tpu_custom_call" | custom-call | tf_op jit(solution)/shard_map/vcycle/pallas_call | solution.py:603
  40.8 0.7 %copy.5 = f32[16,16,256]{2,1,0:T(8,128)} copy(f32[16,16,256]{2,1,0:T(8,128)S(1)} %vcycle.1) | data formatting | bytes 524288

commit v3 on v2

--- a/solution.py
+++ b/solution.py
@@ -13,7 +13,7 @@
     ((dx, dy) for dx in range(GX) for dy in range(NYC) if dx or dy),
     key=lambda o: -(min(o[0], GX - o[0]) + 2 * min(o[1], NYC - o[1])),
 )
-EIGHT = [(0, 1), (0, -1), (1, 1), (1, -1), (-1, 1), (-1, -1), (1, 0), (-1, 0)]
+EIGHT = [(1, 1), (1, -1), (-1, 1), (-1, -1), (0, 1), (0, -1), (1, 0), (-1, 0)]
 
 
 def harmonic(a, b):
@@ -23,12 +23,12 @@
 def mm(a, m):
     hi = a.astype(BF16)
     lo = (a - hi.astype(F32)).astype(BF16)
-    return jnp.dot(hi, m, preferred_element_type=F32) + jnp.dot(lo, m, preferred_element_type=F32)
+    return jnp.dot(jnp.concatenate([hi, lo], axis=1), m, preferred_element_type=F32)
 
 
 def zp(s):
     if len(s) == 1:
-        return (pltpu.roll(s[0], 127, 1),)
+        return (pltpu.roll(s[0], 126 if s[0].shape[0] == 16 else 127, 1),)
     last = lax.broadcasted_iota(jnp.int32, s[0].shape, 1) == 127
     a, b = pltpu.roll(s[0], 127, 1), pltpu.roll(s[1], 127, 1)
     return (jnp.where(last, b, a), jnp.where(last, a, b))
@@ -36,7 +36,7 @@
 
 def zm(s):
     if len(s) == 1:
-        return (pltpu.roll(s[0], 1, 1),)
+        return (pltpu.roll(s[0], 2 if s[0].shape[0] == 16 else 1, 1),)
     first = lax.broadcasted_iota(jnp.int32, s[0].shape, 1) == 0
     a, b = pltpu.roll(s[0], 1, 1), pltpu.roll(s[1], 1, 1)
     return (jnp.where(first, b, a), jnp.where(first, a, b))
@@ -242,7 +242,7 @@
     C1, CX1, CY1, CZ1, W1, B1, VA1, VB1, R1, TP1,
     C2, CX2, CY2, CZ2, W2, B2, VA2, VB2, R2, B2H, V2H,
     C3, B3, V3A, V3B, K3, C4, B4, V4A, V4B, K4, GC, GB,
-    MR, M3, MP1, MP2, MP3, ROWS,
+    MR, M3, MP1, MP3, ROWS,
     lsem, e0s, e0r, c1s, c1r, b1s, b1r, h0s, h0r, h2s, h2r, cg, bg,
 ):
     gx, gy = lax.axis_index("gx"), lax.axis_index("gy")
@@ -287,8 +287,8 @@
         pl.semaphore_signal(barrier, inc=1, device_id=along_z(k), device_id_type=MESH)
         return carry
 
+    lax.fori_loop(1, NZC, greet_z, 0)
     lax.fori_loop(1, GX * NYC, greet_plane, 0)
-    lax.fori_loop(1, NZC, greet_z, 0)
 
     pl.semaphore_wait(barrier, len(EIGHT) + GX * NYC - 1 + NZC - 1)
 
@@ -317,39 +317,38 @@
     e0c = exchange(C0, (3, 4), 16, 3, e0s.at[0], e0r.at[0], 2)
     e0v = exchange(V0, (3, 4), 16, 3, e0s.at[1], e0r.at[1], 2)
     e0b = exchange(B0, (3, 4), 16, 2, e0s.at[2], e0r.at[2], 1)
-    for faces in ((0, 1), (2, 3, 4, 5), (6, 7)):
+    for first in (0, 4, 6):
         for n, copies in enumerate((e0c, e0v, e0b)):
-            if faces[0] == 0:
+            if first == 0:
                 loads[2 * n].wait()
                 loads[2 * n + 1].wait()
-            for i in faces:
-                copies[i].start()
+            for copy in copies[first : first + 4 if first == 0 else first + 2]:
+                copy.start()
 
     def matrix(rows, columns, rule):
-        r = lax.broadcasted_iota(jnp.int32, (rows, columns), 0)
-        c = lax.broadcasted_iota(jnp.int32, (rows, columns), 1)
+        r = lax.broadcasted_iota(jnp.int32, (2 * rows, columns), 0) % rows
+        c = lax.broadcasted_iota(jnp.int32, (2 * rows, columns), 1)
         return jnp.where(rule(r, c), 1.0, 0.0).astype(BF16)
 
-    MR[0:256] = matrix(256, 128, lambda r, c: r // 2 == c)
-    MR[256:384] = matrix(128, 128, lambda r, c: r // 2 == c % 64)
-    M3[...] = matrix(128, 128, lambda r, c: (r < 64) & (r // 2 == c % 32))
+    MR[...] = matrix(256, 128, lambda r, c: r // 2 == c)
+    M3[...] = matrix(128, 128, lambda r, c: (r % 2 == 0) & (r // 4 == c % 32))
     MP1[...] = matrix(128, 256, lambda r, c: r == c // 2)
-    MP2[...] = matrix(128, 128, lambda r, c: r == c // 2)
-    MP3[...] = matrix(128, 512, lambda r, c: (r // 32 == c // 128) & (r % 32 == (c % 64) // 2))
+    MP3[...] = matrix(128, 512, lambda r, c: (r // 32 == c // 128) & (r % 32 == (c % 128) // 4))
 
     def restrict_zero(ref, scale):
         pairs = [
             jnp.concatenate([ref[3 + 2 * k, h, 4:20] + ref[4 + 2 * k, h, 4:20] for h in range(2)], axis=1)
             for k in range(8)
         ]
-        TR[0:8, 0:16] = mm(jnp.concatenate(pairs, axis=0), MR[0:256]).reshape(8, 16, 128)
+        TR[0:8, 0:16] = mm(jnp.concatenate(pairs, axis=0), MR[...]).reshape(8, 16, 128)
         return (TR[0:8, pl.ds(0, 8, stride=2), :] + TR[0:8, pl.ds(1, 8, stride=2), :]) * scale
 
     def restrict_one(ref, x0, count, y0, rows, scale):
-        pairs = [ref[x0 + 2 * k, y0 : y0 + rows] + ref[x0 + 1 + 2 * k, y0 : y0 + rows] for k in range(count)]
-        TR[0:count, 0:rows] = mm(jnp.concatenate(pairs, axis=0), MR[256:384]).reshape(count, rows, 128)
+        for k in range(count):
+            TR[k, 0:rows] = ref[x0 + 2 * k, y0 : y0 + rows] + ref[x0 + 1 + 2 * k, y0 : y0 + rows]
         half = rows // 2
-        return (TR[0:count, pl.ds(0, half, stride=2), :] + TR[0:count, pl.ds(1, half, stride=2), :]) * scale
+        s = (TR[0:count, pl.ds(0, half, stride=2), :] + TR[0:count, pl.ds(1, half, stride=2), :]) * scale
+        return s + jnp.where(lane(s.shape) % 2 == 0, pltpu.roll(s, 127, 2), pltpu.roll(s, 1, 2))
 
     def restrict_two(ref, scale):
         pairs = jnp.concatenate([ref[4] + ref[5], ref[6] + ref[7]], axis=0)
@@ -394,14 +393,14 @@
 
     C1[8:16, 8:16] = restrict_zero(C0, 0.125 * 0.25)
     c1 = exchange(C1, (8, 8), 8, 8, c1s, c1r)
-    for copy in c1:
-        copy.start()
     C2[4:8, 4:8] = restrict_one(C1, 8, 4, 8, 8, 0.125 * 0.25)
     GC[NZC // 2, yc, pl.ds(gx, 1), :] = restrict_two(C2, 0.125 * 0.25)
     start_z(GC, cg)
 
     for copy in e0c:
         copy.wait_recv()
+    for copy in c1:
+        copy.start()
     coefficients(C0, CX0, CY0, CZ0, W0, 22)
     for copy in e0v + e0b:
         copy.wait_recv()
@@ -525,9 +524,8 @@
         rows = VA2[2 + k, 0:12, :]
         TP1[k, pl.ds(0, 12, stride=2), :] = rows
         TP1[k, pl.ds(1, 12, stride=2), :] = rows
-    TR[0:8] = mm(TP1[...].reshape(8 * 24, 128), MP2[...]).reshape(8, 24, 128)
     for x in range(5, 19):
-        VA1[x] = VB1[x] + TR[x // 2 - 2]
+        VA1[x] = VB1[x] + TP1[x // 2 - 2]
     sweep(VA1, R1, *one, W1, 6, 18)
     sweep(R1, VA1, *one, W1, 7, 17)
 
@@ -591,7 +589,7 @@
         + [vmem(GY + 2, GX, 128)] * 4
         + [vmem(8, GY, GX, 128)]
         + [vmem(NZC, NYC, GX, 128)] * 2
-        + [half(384, 128), half(128, 128), half(128, 256), half(128, 128), half(128, 512)]
+        + [half(512, 128), half(256, 128), half(256, 256), half(256, 512)]
         + [vmem(GX * NYC - 1, NZC, 128)]
         + [dma((6,)), dma((3, 8)), dma((3, 8))]
         + [dma((8,))] * 6

time: 41.5 us -> 40 us (0.964)
  Pallas kernels: 40.8 us -> 39.2 us
    pallas_call x1, Pallas kernels: 40.8 us -> 39.2 us  [step(): pl.pallas_call(kernel, out_shape=jax.ShapeDtypeStruct(source.shape, F32),...]
where the time goes in v3:
time: 40 us; the launch traced here: 39.9 us
  Pallas kernels  39.2 us (98%)
  local copies, waits for them, and re-layouts  0.71 us (2%)
    pallas_call x1, Pallas kernels, step(): pl.pallas_call(kernel, out_shape=jax.ShapeDtypeStruct(source.shape, F32),...  39.2 us

profile of v3, /device:TPU:1, one launch (start us, length us, event | category | flops | bytes accessed | tf_op | source)
XLA Modules:
  0.0 39.9 jit_solution(10411451762220986817)
XLA Ops:
  0.0 39.2 %vcycle.1 = f32[16,16,256]{2,1,0:T(8,128)S(1)} custom-call(f32[16,16,256]{2,1,0:T(8,128)} %src_ref.1, f32[16,16,256]{2,1,0:T(8,128)} %cond_ref.1, f32[16,16,256]{2,1,0:T(8,128)} %guess_ref.1), custom_call_target="tpu_custom_call" | custom-call | tf_op jit(solution)/shard_map/vcycle/pallas_call | solution.py:601
  39.2 0.7 %copy.5 = f32[16,16,256]{2,1,0:T(8,128)} copy(f32[16,16,256]{2,1,0:T(8,128)S(1)} %vcycle.1) | data formatting | bytes 524288

commit v4 on v3

--- a/solution.py
+++ b/solution.py
@@ -14,6 +14,7 @@
     key=lambda o: -(min(o[0], GX - o[0]) + 2 * min(o[1], NYC - o[1])),
 )
 EIGHT = [(1, 1), (1, -1), (-1, 1), (-1, -1), (0, 1), (0, -1), (1, 0), (-1, 0)]
+Z_FAR_FIRST = (4, 3, 5, 2, 6, 1, 7)
 
 
 def harmonic(a, b):
@@ -251,9 +252,6 @@
     def beside(dx, dy):
         return (lax.rem(gx + dx + GX, GX), lax.rem(gy + dy + GY, GY))
 
-    def in_plane(k):
-        return (lax.rem(gx + lax.div(k, NYC), GX), zc * NYC + lax.rem(yc + lax.rem(k, NYC), NYC))
-
     def along_z(k):
         return (gx, lax.rem(zc + k, NZC) * NYC + yc)
 
@@ -272,23 +270,18 @@
                     lsem.at[2 * i + h],
                 )
             )
-    for copy in loads:
-        copy.start()
-
     barrier = pltpu.get_barrier_semaphore()
     for dx, dy in EIGHT:
         pl.semaphore_signal(barrier, inc=1, device_id=beside(dx, dy), device_id_type=MESH)
 
-    def greet_plane(k, carry):
-        pl.semaphore_signal(barrier, inc=1, device_id=in_plane(k), device_id_type=MESH)
-        return carry
-
-    def greet_z(k, carry):
+    columns = [lax.rem(gx + d, GX) for d in range(GX)]
+    rows = [zc * NYC + lax.rem(yc + d, NYC) for d in range(NYC)]
+    for dx, dy in FAR_FIRST:
+        pl.semaphore_signal(barrier, inc=1, device_id=(columns[dx], rows[dy]), device_id_type=MESH)
+    for k in Z_FAR_FIRST:
         pl.semaphore_signal(barrier, inc=1, device_id=along_z(k), device_id_type=MESH)
-        return carry
-
-    lax.fori_loop(1, NZC, greet_z, 0)
-    lax.fori_loop(1, GX * NYC, greet_plane, 0)
+    for copy in loads:
+        copy.start()
 
     pl.semaphore_wait(barrier, len(EIGHT) + GX * NYC - 1 + NZC - 1)
 
@@ -367,10 +360,10 @@
 
     def plane_copy(ref, dx, dy, sems):
         part = ref.at[:, yc, pl.ds(gx, 1), :]
-        return remote(part, part, sems.at[2], sems.at[3], in_plane(dx * NYC + dy))
+        return remote(part, part, sems.at[2], sems.at[3], (columns[dx], rows[dy]))
 
     def start_z(ref, sems):
-        for k in (4, 3, 5, 2, 6, 1, 7):
+        for k in Z_FAR_FIRST:
             z_copy(ref, k, sems).start()
 
     def start_plane(ref, sems):
@@ -477,21 +470,21 @@
     landed_plane(bg)
 
     b3 = GB[...].reshape(GY, GX, 128)
+    mean = jnp.sum(jnp.sum(b3, axis=0), keepdims=True) * (1.0 / (GY * GX * 128))
     B3[1 : GY + 1] = b3
     V3A[1 : GY + 1] = K3[7] * b3
     wrap_rows(V3A)
-    whole_sweep(THREE, V3A, V3B, B3, K3)
+    whole_sweep(THREE, V3A, V3B, B3, K3, 5, 31)
 
     def residual(lo, hi, v, s):
         r = B3[lo + 1 : hi + 1] + s - K3[6, lo:hi] * v
         B4[lo + 1 : hi + 1] = coarsen_lanes(r) * 0.125
 
-    whole_sum(THREE, V3B, K3, residual, 0, GY)
-
-    b4 = B4[1 : GY + 1]
-    b4 = b4 - jnp.sum(jnp.sum(b4, axis=0), keepdims=True) * (1.0 / (GY * GX * 128))
-    B4[1 : GY + 1] = b4
-    V4A[7:31] = K4[7, 6:30] * b4[6:30]
+    whole_sum(THREE, V3B, K3, residual, 6, 30)
+
+    b4 = B4[7:31] - mean
+    B4[7:31] = b4
+    V4A[7:31] = K4[7, 6:30] * b4
     here, there = V4A, V4B
     for i in range(7):
         whole_sweep(FOUR, here, there, B4, K4, 7 + i, 29 - i)
@@ -521,18 +514,18 @@
     sweep(R2, VA2, *two, W2, 2, 10)
 
     for k in range(8):
-        rows = VA2[2 + k, 0:12, :]
-        TP1[k, pl.ds(0, 12, stride=2), :] = rows
-        TP1[k, pl.ds(1, 12, stride=2), :] = rows
+        cells = VA2[2 + k, 0:12, :]
+        TP1[k, pl.ds(0, 12, stride=2), :] = cells
+        TP1[k, pl.ds(1, 12, stride=2), :] = cells
     for x in range(5, 19):
         VA1[x] = VB1[x] + TP1[x // 2 - 2]
     sweep(VA1, R1, *one, W1, 6, 18)
     sweep(R1, VA1, *one, W1, 7, 17)
 
     for k in range(10):
-        rows = VA1[7 + k, 7:17, :]
-        TP0[k, pl.ds(2, 10, stride=2), :] = rows
-        TP0[k, pl.ds(3, 10, stride=2), :] = rows
+        cells = VA1[7 + k, 7:17, :]
+        TP0[k, pl.ds(2, 10, stride=2), :] = cells
+        TP0[k, pl.ds(3, 10, stride=2), :] = cells
     u = mm(TP0[...].reshape(10 * 24, 128), MP1[...])
     for h in range(2):
         PE0[:, h] = u[:, 128 * h : 128 * h + 128].reshape(10, 24, 128)

time: 40 us -> 39 us (0.975)
  Pallas kernels: 39.2 us -> 38.2 us
    pallas_call x1, Pallas kernels: 39.2 us -> 38.2 us  [step(): pl.pallas_call(kernel, out_shape=jax.ShapeDtypeStruct(source.shape, F32),...]
where the time goes in v4:
time: 39 us; the launch traced here: 38.9 us
  Pallas kernels  38.2 us (98%)
  local copies, waits for them, and re-layouts  0.71 us (2%)
    pallas_call x1, Pallas kernels, step(): pl.pallas_call(kernel, out_shape=jax.ShapeDtypeStruct(source.shape, F32),...  38.2 us

profile of v4, /device:TPU:1, one launch (start us, length us, event | category | flops | bytes accessed | tf_op | source)
XLA Modules:
  0.0 38.9 jit_solution(3301821024901387802)
XLA Ops:
  0.0 38.2 %vcycle.1 = f32[16,16,256]{2,1,0:T(8,128)S(1)} custom-call(f32[16,16,256]{2,1,0:T(8,128)} %src_ref.1, f32[16,16,256]{2,1,0:T(8,128)} %cond_ref.1, f32[16,16,256]{2,1,0:T(8,128)} %guess_ref.1), custom_call_target="tpu_custom_call" | custom-call | tf_op jit(solution)/shard_map/vcycle/pallas_call | solution.py:594
  38.2 0.7 %copy.5 = f32[16,16,256]{2,1,0:T(8,128)} copy(f32[16,16,256]{2,1,0:T(8,128)S(1)} %vcycle.1) | data formatting | bytes 524288

commit v5 on v4

--- a/solution.py
+++ b/solution.py
@@ -420,8 +420,6 @@
             ((-1, -1), (3, 19, 1), (4, 20, 1)),
         ))
     ]
-    for copy in h0:
-        copy.start()
 
     landed_z(cg)
     start_plane(GC, cg)
@@ -451,6 +449,8 @@
     flux_loop(VB2, *two, 4, 8, lambda x, v, r: put(R2, x, r))
     GB[NZC // 2, yc, pl.ds(gx, 1), :] = restrict_two(R2, 0.125)
     start_z(GB, bg)
+    for copy in h0:
+        copy.start()
     B2H[4:8, 4:8] = B2[4:8, 4:8]
     V2H[4:8, 4:8] = VB2[4:8, 4:8]
     h2 = exchange(B2H, (4, 4), 4, 4, h2s.at[0], h2r.at[0]) + exchange(V2H, (4, 4), 4, 4, h2s.at[1], h2r.at[1])

time: 39 us -> 38.9 us (level)
  no operation moved by 1% of the time
where the time goes in v5:
time: 38.9 us; the launch traced here: 38.8 us
  Pallas kernels  38.1 us (98%)
  local copies, waits for them, and re-layouts  0.71 us (2%)
    pallas_call x1, Pallas kernels, step(): pl.pallas_call(kernel, out_shape=jax.ShapeDtypeStruct(source.shape, F32),...  38.1 us

profile of v5, /device:TPU:1, one launch (start us, length us, event | category | flops | bytes accessed | tf_op | source)
XLA Modules:
  0.0 38.8 jit_solution(7762308701122700465)
XLA Ops:
  0.0 38.1 %vcycle.1 = f32[16,16,256]{2,1,0:T(8,128)S(1)} custom-call(f32[16,16,256]{2,1,0:T(8,128)} %src_ref.1, f32[16,16,256]{2,1,0:T(8,128)} %cond_ref.1, f32[16,16,256]{2,1,0:T(8,128)} %guess_ref.1), custom_call_target="tpu_custom_call" | custom-call | tf_op jit(solution)/shard_map/vcycle/pallas_call | solution.py:594
  38.1 0.7 %copy.5 = f32[16,16,256]{2,1,0:T(8,128)} copy(f32[16,16,256]{2,1,0:T(8,128)S(1)} %vcycle.1) | data formatting | bytes 524288

commit v6 on v4

--- a/solution.py
+++ b/solution.py
@@ -457,6 +457,8 @@
     for copy in h2:
         copy.start()
 
+    landed_z(bg)
+    start_plane(GB, bg)
     landed_plane(cg)
     C3[1 : GY + 1] = GC[...].reshape(GY, GX, 128)
     wrap_rows(C3)
@@ -465,8 +467,6 @@
     wrap_rows(C4)
     whole_coefficients(FOUR, C4, K4)
 
-    landed_z(bg)
-    start_plane(GB, bg)
     landed_plane(bg)
 
     b3 = GB[...].reshape(GY, GX, 128)

time: 39 us -> 39 us (level)
  no operation moved by 1% of the time
where the time goes in v6:
time: 39 us; the launch traced here: 38.9 us
  Pallas kernels  38.2 us (98%)
  local copies, waits for them, and re-layouts  0.71 us (2%)
    pallas_call x1, Pallas kernels, step(): pl.pallas_call(kernel, out_shape=jax.ShapeDtypeStruct(source.shape, F32),...  38.2 us

profile of v6, /device:TPU:1, one launch (start us, length us, event | category | flops | bytes accessed | tf_op | source)
XLA Modules:
  0.0 38.9 jit_solution(13972199057219213180)
XLA Ops:
  0.0 38.2 %vcycle.1 = f32[16,16,256]{2,1,0:T(8,128)S(1)} custom-call(f32[16,16,256]{2,1,0:T(8,128)} %src_ref.1, f32[16,16,256]{2,1,0:T(8,128)} %cond_ref.1, f32[16,16,256]{2,1,0:T(8,128)} %guess_ref.1), custom_call_target="tpu_custom_call" | custom-call | tf_op jit(solution)/shard_map/vcycle/pallas_call | solution.py:594
  38.2 0.7 %copy.5 = f32[16,16,256]{2,1,0:T(8,128)} copy(f32[16,16,256]{2,1,0:T(8,128)S(1)} %vcycle.1) | data formatting | bytes 524288
